TPU v7x, 128 devices: a whole 4x4x4 slice. The times are simulated.
128 devices in a mesh: freq: 8 (over y, core), space: 16 (over x, z).
Axes of the slice: x: 4, y: 4, z: 4, core: 2. Of those that a mesh axis runs over, the one named last changes fastest.
Arguments:
- traces: float32 [1024, 512, 256], P(('freq', 'space')), may hold values from -50 to 50
- probes: float32 [16, 128, 64], P('freq'), may hold values from -0.5 to 0.5
Outputs:
- denoised: float32 [1024, 512, 256], P(('freq', 'space'))
All inputs are finite; a program needn't handle non-finite values.
Results may differ from a plain program's by a relative error of at most 0.000092.
Values sent between devices are 32-bit elements; how exact they have to be, the bound alone decides.
A program may use at most 128 MiB of HBM per device.

v0:
```python
import jax
import jax.numpy as jnp
from jax import lax
from jax.sharding import PartitionSpec as P

NT = 1024
BAND_LO = 16


HIGHEST_PRECISION = lax.Precision.HIGHEST


def in_blocks(array, dim, peers):
    before, after = (array.shape[:dim], array.shape[dim + 1 :])
    return jnp.moveaxis(array.reshape(*before, peers, -1, *after), dim, 0)


def sent_and_summed(array, axis, dim):
    peers = lax.axis_size(axis)
    tiles = lax.all_to_all(in_blocks(array, dim, peers), axis, 0, 0, tiled=True)
    return jnp.sum(tiles, axis=0)


def copy_for_each(array, axis):
    peers = lax.axis_size(axis)
    return lax.all_to_all(
        jnp.broadcast_to(array[None], (peers, *array.shape)), axis, 0, 0, tiled=True
    )


def in_order(tiles, dim):
    shape = list(tiles.shape[1:])
    shape[dim] *= tiles.shape[0]
    return jnp.moveaxis(tiles, 0, dim).reshape(shape)


def gather_directly(array, axis, dim):
    tiles = copy_for_each(array, axis)
    return in_order(tiles, dim)


def wave_table(freq_ids, time_ids, period, factor):
    phase = (freq_ids[:, None] * time_ids[None, :] % period).astype(jnp.float32) * (
        2.0 * jnp.pi / period
    )
    return jnp.stack([jnp.cos(phase), -jnp.sin(phase)]) * factor


def hankel(spectrum, window, columns):
    width = spectrum.shape[-1]
    tiled = jnp.tile(spectrum, (1, 1, window + 1))[:, :, : window * (width + 1)]
    return tiled.reshape(spectrum.shape[0], spectrum.shape[1], window, width + 1)[:, :, :, :columns]


def diag_mean(blocks, width):
    halves, channels, window, columns = blocks.shape
    padded = jnp.pad(blocks, ((0, 0), (0, 0), (0, 0), (0, width + 1 - columns)))
    flat_rows = padded.reshape(halves, channels, window * (width + 1))
    flat_rows = jnp.pad(flat_rows, ((0, 0), (0, 0), (0, width - window)))
    totals = flat_rows.reshape(halves, channels, window + 1, width).sum(axis=2)
    position = jnp.arange(width, dtype=jnp.int32)
    counts = jnp.minimum(jnp.minimum(position + 1, width - position), min(window, columns))
    return totals / counts.astype(jnp.float32)


def assemble(gram_raw, cross_raw):
    half = gram_raw.shape[-1] // 2
    diagonal_part = gram_raw[..., :half, :half] + gram_raw[..., half:, half:]
    skew_part = gram_raw[..., half:, :half] - gram_raw[..., :half, half:]
    gram_matrix = jnp.concatenate(
        [
            jnp.concatenate([diagonal_part, skew_part], -1),
            jnp.concatenate([-skew_part, diagonal_part], -1),
        ],
        -2,
    )
    real_rows = cross_raw[..., 0, :, :]
    imag_rows = cross_raw[..., 1, :, :]
    cross_terms = jnp.concatenate(
        [
            real_rows[..., :half, :] + imag_rows[..., half:, :],
            imag_rows[..., :half, :] - real_rows[..., half:, :],
        ],
        -2,
    )
    return (gram_matrix, cross_terms)


def solve_one(factor_rows, right_rows):
    return jax.scipy.linalg.cho_solve((factor_rows, True), right_rows)


def first_pass(slice_pair):
    spectrum, probe = slice_pair
    width = spectrum.shape[-1]
    window = width // 2 + 1
    columns = width // 2
    channels = spectrum.shape[1]
    hankel_rows = hankel(spectrum, window, columns).reshape(2, channels * window, columns)
    sketch_basis = jnp.einsum(
        "qrp,pk->rqk", hankel_rows, probe, precision=HIGHEST_PRECISION
    ).reshape(channels * window, 2 * probe.shape[1])
    gram_raw = jnp.dot(sketch_basis.T, sketch_basis, precision=HIGHEST_PRECISION)
    cross_raw = jnp.einsum("rk,qrp->qkp", sketch_basis, hankel_rows, precision=HIGHEST_PRECISION)
    return (sketch_basis, gram_raw, cross_raw)


def body(traces, probes):
    time_slab = lax.all_to_all(traces, "space", split_axis=1, concat_axis=0, tiled=True)
    time_local = time_slab.shape[0]
    channels = time_slab.shape[1]
    width = time_slab.shape[2]
    freq_local = probes.shape[0]
    freq_total = freq_local * lax.axis_size("freq")
    time_ids = lax.axis_index("freq") * time_local + jnp.arange(time_local, dtype=jnp.int32)
    freq_ids = (
        BAND_LO + jnp.int32(0) + jnp.arange(freq_local * lax.axis_size("freq"), dtype=jnp.int32)
    )
    wave_rows = wave_table(freq_ids, time_ids, NT, NT ** (-0.5))
    spectra = sent_and_summed(
        jnp.einsum("qft,tcx->fqcx", wave_rows, time_slab, precision=HIGHEST_PRECISION), "freq", 0
    )
    sketch_basis, gram_raw, cross_raw = lax.map(first_pass, (spectra, probes))
    gram_sum, cross_sum = lax.psum((gram_raw, cross_raw), "space")
    gram_matrix, cross_terms = assemble(gram_sum, cross_sum)
    lower_factor = jnp.linalg.cholesky(gram_matrix)
    coeffs = jax.vmap(solve_one)(lower_factor, cross_terms)
    window = width // 2 + 1
    columns = width // 2

    def second_pass(slice_pair):
        basis_rows, coeff_rows = slice_pair
        half = coeff_rows.shape[0] // 2
        real_part = coeff_rows[:half]
        imag_part = coeff_rows[half:]
        mixing = jnp.stack(
            [
                jnp.concatenate([real_part, -imag_part], 0),
                jnp.concatenate([imag_part, real_part], 0),
            ]
        )
        rebuilt = jnp.einsum("rk,qkp->qrp", basis_rows, mixing, precision=HIGHEST_PRECISION)
        return diag_mean(rebuilt.reshape(2, channels, window, columns), width)

    clean = lax.map(second_pass, (sketch_basis, coeffs))
    start_volume = jnp.zeros((time_local, channels, width), jnp.float32)
    shard_piece = gather_directly(clean, "freq", 0)
    freq_ids = BAND_LO + jnp.int32(0) + jnp.arange(shard_piece.shape[0], dtype=jnp.int32)
    wave_rows = wave_table(freq_ids, time_ids, NT, (2.0 / freq_total) ** 0.5)
    volume = start_volume + jnp.einsum(
        "qft,fqcx->tcx", wave_rows, shard_piece, precision=HIGHEST_PRECISION
    )
    return lax.all_to_all(volume, "space", split_axis=0, concat_axis=1, tiled=True)


def solution(mesh):
    in_specs = (P(("freq", "space"), None, None), P("freq", None, None))
    out_specs = P(("freq", "space"), None, None)
    return jax.shard_map(body, mesh=mesh, in_specs=in_specs, out_specs=out_specs, check_vma=False)
```

profile of v0, /device:TPU:1, one launch (start us, length us, event | category | flops | bytes accessed | tf_op | source)
XLA Modules:
  0.0 567.4 jit_solution(8227421941552182620)
XLA Ops:
  6.5 6.6 %copy.35 = f32[8,512,256]{2,0,1:T(8,128)} copy(f32[8,512,256]{2,1,0:T(8,128)} %param.6) | data formatting | bytes 8388608 | tf_op args[0]
  13.2 8.5 %all-to-all-start = ((f32[8,512,256]{2,0,1:T(8,128)}), f32[8,512,256]{2,0,1:T(8,128)}, u32[]{:S(2)}, u32[]{:S(2)}) async-start(f32[8,512,256]{2,0,1:T(8,128)} %copy.35), calls=%async_computation | async-start | bytes 8388608 | tf_op jit(solution)/shard_map/all_to_all | solution.py:109
  21.8 61.3 %all-to-all-done = f32[8,512,256]{2,0,1:T(8,128)} async-done(((f32[8,512,256]{2,0,1:T(8,128)}), f32[8,512,256]{2,0,1:T(8,128)}, u32[]{:S(2)}, u32[]{:S(2)}) %all-to-all-start) | async-done | bytes 4194336 | tf_op jit(solution)/shard_map/all_to_all | solution.py:109
  89.3 6.9 %all-to-all-start.1 = ((f32[8,2,2,32,256]{4,1,3,2,0:T(2,128)}), f32[8,2,2,32,256]{4,1,3,2,0:T(2,128)S(1)}, u32[]{:S(2)}, u32[]{:S(2)}) async-start(f32[8,2,2,32,256]{4,1,3,2,0:T(2,128)} %copy.37), calls=%async_computation.1 | async-start | bytes 2097152 | tf_op jit(solution)/shard_map/all_to_all | solution.py:20
  96.2 15.1 %all-to-all-done.1 = f32[8,2,2,32,256]{4,1,3,2,0:T(2,128)S(1)} async-done(((f32[8,2,2,32,256]{4,1,3,2,0:T(2,128)}), f32[8,2,2,32,256]{4,1,3,2,0:T(2,128)S(1)}, u32[]{:S(2)}, u32[]{:S(2)}) %all-to-all-start.1) | async-done | bytes 1048608 | tf_op jit(solution)/shard_map/all_to_all | solution.py:20
  111.7 124.3 %while.26 = (s32[]{:T(128)}, f32[2,4128,128]{2,1,0:T(8,128)}, f32[2,128,128]{1,2,0:T(8,128)S(1)}, f32[2,2,128,128]{3,2,0,1:T(8,128)S(1)}, f32[2,128,64]{1,2,0:T(...) while((s32[]{:T(128)}, f32[2,4128,128]{2,1,0:T(8,128)}, f32[2,128,128]{1,2,0:T(8,128)S(1)}, ...), condition=%wide.region_2.3_spmd, body=%wide.region_1.2_spmd.sunk | while | flops 3246391296 | bytes 102892656 | solution.py:123
  116.3 9.5 %tile.14 = f32[2,32,33280]{2,1,0:T(8,128)} reshape(f32[2,32,130,256]{3,2,1,0:T(8,128)} %tile.13) | data formatting | bytes 17039360 | tf_op jit(solution)/shard_map/while/body/eval_jaxpr/tile | solution.py:51
  125.8 12.6 %reshape.234 = f32[2,32,129,257]{3,2,1,0:T(8,128)} reshape(f32[2,32,33153]{2,1,0:T(8,128)} %bitcast.135) | data formatting | bytes 16974336 | tf_op jit(solution)/shard_map/while/body/eval_jaxpr/reshape | solution.py:52
  147.9 6.6 %fusion.71 = f32[64,2,4128]{2,0,1:T(8,128)S(1)} fusion(f32[2,4128,128]{2,1,0:T(8,128)} %reshape.235, f32[2,128,64]{1,2,0:T(8,128)S(1)} %get-tuple-element.247, s32[]{:T(128)} %get-tuple-element.236), kind=kOutput, calls=%fused_computation.4.clone.1 | convolution fusion | flops 811597824 | bytes 6373380 | tf_op jit(solution)/shard_map/while/body/eval_jaxpr/qrp,pk->rqk/dot_general | solution.py:100
  154.5 7.1 %convolution_bitcast_fusion.6 = f32[1,2,128,128]{2,3,1,0:T(8,128)S(1)} fusion(f32[2,4128,128]{2,1,0:T(8,128)S(1)} %copy-done, f32[4128,128,1]{0,1,2:T(8,128)S(1)} %bitcast.132), kind=kOutput, calls=%fused_computation.clone.1 | convolution fusion | flops 1623195648 | bytes 6471680 | tf_op jit(solution)/shard_map/while/body/eval_jaxpr/rk,qrp->qkp/dot_general | solution.py:104
  173.1 9.5 %tile.14 = f32[2,32,33280]{2,1,0:T(8,128)} reshape(f32[2,32,130,256]{3,2,1,0:T(8,128)} %tile.13) | data formatting | bytes 17039360 | tf_op jit(solution)/shard_map/while/body/eval_jaxpr/tile | solution.py:51
  182.6 12.6 %reshape.234 = f32[2,32,129,257]{3,2,1,0:T(8,128)} reshape(f32[2,32,33153]{2,1,0:T(8,128)} %bitcast.135) | data formatting | bytes 16974336 | tf_op jit(solution)/shard_map/while/body/eval_jaxpr/reshape | solution.py:52
  204.7 6.6 %fusion.71 = f32[64,2,4128]{2,0,1:T(8,128)S(1)} fusion(f32[2,4128,128]{2,1,0:T(8,128)} %reshape.235, f32[2,128,64]{1,2,0:T(8,128)S(1)} %get-tuple-element.247, s32[]{:T(128)} %get-tuple-element.236), kind=kOutput, calls=%fused_computation.4.clone.1 | convolution fusion | flops 811597824 | bytes 6373380 | tf_op jit(solution)/shard_map/while/body/eval_jaxpr/qrp,pk->rqk/dot_general | solution.py:100
  211.3 7.1 %convolution_bitcast_fusion.6 = f32[1,2,128,128]{2,3,1,0:T(8,128)S(1)} fusion(f32[2,4128,128]{2,1,0:T(8,128)S(1)} %copy-done, f32[4128,128,1]{0,1,2:T(8,128)S(1)} %bitcast.132), kind=kOutput, calls=%fused_computation.clone.1 | convolution fusion | flops 1623195648 | bytes 6471680 | tf_op jit(solution)/shard_map/while/body/eval_jaxpr/rk,qrp->qkp/dot_general | solution.py:104
  236.9 86.1 %all-reduce.5.cloned.1.call-done = (f32[2,2,128,128]{3,2,0,1:T(8,128)}, f32[2,128,128]{1,2,0:T(8,128)}) async-done(((f32[2,2,128,128]{3,2,0,1:T(8,128)}, f32[2,128,128]{1,2,0:T(8,128)}), (f32[2,2,128,128]{3,2,0,1:T(8,128)}, f32[2,128,128]{1,2,0:T(8,128)})) %all-reduce.5.cloned.1.call-update) | async-done | bytes 393232 | tf_op jit(solution)/shard_map/psum | solution.py:124
  324.3 23.5 %custom-call.11 = f32[2,128,128]{2,1,0:T(8,128)S(1)} custom-call(f32[2,128,128]{2,1,0:T(8,128)S(1)} %fusion.28), custom_call_target="Cholesky" | custom-call | tf_op jit(solution)/shard_map/jit(cholesky)/cholesky | solution.py:126
  348.0 19.7 %custom-call.12 = f32[2,1,128,128]{2,3,1,0:T(8,128)S(1)} custom-call(f32[2,1,128,128]{3,2,1,0:T(8,128)S(1)} %select_bitcast_fusion), custom_call_target="InvertDiagBlocksLowerTriangular" | custom-call | tf_op jit(solution)/shard_map/vmap(jit(_cho_solve))/triangular_solve | solution.py:90
  369.4 107.1 %while.27 = (s32[]{:T(128)}, f32[2,2,32,256]{3,0,1,2:T(2,128)S(1)}, f32[2,128,128]{2,1,0:T(8,128)S(1)}, f32[2,4128,128]{2,1,0:T(8,128)}, s32[]{:T(128)}, /*index=5*/s32[]{:T(128)}, s32[]{}, f32[]{:T(128)}) while((s32[]{:T(128)}, f32[2,2,32,256]{3,0,1,2:T(2,128)S(1)}, f32[2,128,128]{2,1,0:T(8,128)S(1)}, f32[2,4128,128]{2,1,0:T(8,128)}, ...), condition=%wide.region_9.10_spmd, body=%wide.region_7.9_spmd.sunk | while | flops 1625400576 | bytes 88034936 | solution.py:145
  369.5 7.0 %convolution_bitcast_fusion.7 = f32[2,4128,128]{2,1,0:T(8,128)} fusion(f32[2,4128,128]{2,1,0:T(8,128)} %get-tuple-element.269, s32[]{:T(128)} %get-tuple-element.258, f32[1,128,128]{2,1,0:T(8,128)S(1)} %get-tuple-element.227, f32[1,128,128]{2,1,0:T(8,128)S(1)} %get-tuple-element.228), kind=kOutput, calls=%fused_computation.11.clone.1 | convolution fusion | flops 1623228416 | bytes 6472192 | tf_op jit(solution)/shard_map/while/body/eval_jaxpr/rk,qkp->qrp/dot_general | solution.py:142
  376.5 4.8 reshape.236
  381.3 7.9 %pad.84 = f32[2,32,129,257]{3,2,1,0:T(8,128)} pad(f32[2,32,129,128]{3,2,1,0:T(8,128)} %reshape.236, f32[]{:T(128)} %constant.140.clone.1..sunk), padding=0_0x0_0x0_0x0_129 | pad | bytes 12714244 | tf_op jit(solution)/shard_map/while/body/eval_jaxpr/jit(_pad)/pad | solution.py:57
  389.2 11.6 %reshape.237 = f32[2,32,33153]{2,1,0:T(8,128)} reshape(f32[2,32,129,257]{3,2,1,0:T(8,128)} %pad.84) | data formatting | bytes 16974336 | tf_op jit(solution)/shard_map/while/body/eval_jaxpr/reshape | solution.py:58
  400.8 7.3 %pad.85 = f32[2,32,33280]{2,1,0:T(8,128)} pad(f32[2,32,33153]{2,1,0:T(8,128)} %reshape.237, f32[]{:T(128)} %constant.140.clone.1..sunk), padding=0_0x0_0x0_127 | pad | bytes 17006852 | tf_op jit(solution)/shard_map/while/body/eval_jaxpr/jit(_pad)/pad | solution.py:59
  408.2 9.4 %reshape.238 = f32[2,32,130,256]{3,2,1,0:T(8,128)} reshape(f32[2,32,33280]{2,1,0:T(8,128)} %pad.85) | data formatting | bytes 17039360 | tf_op jit(solution)/shard_map/while/body/eval_jaxpr/reshape | solution.py:60
  423.0 7.0 %convolution_bitcast_fusion.7 = f32[2,4128,128]{2,1,0:T(8,128)} fusion(f32[2,4128,128]{2,1,0:T(8,128)} %get-tuple-element.269, s32[]{:T(128)} %get-tuple-element.258, f32[1,128,128]{2,1,0:T(8,128)S(1)} %get-tuple-element.227, f32[1,128,128]{2,1,0:T(8,128)S(1)} %get-tuple-element.228), kind=kOutput, calls=%fused_computation.11.clone.1 | convolution fusion | flops 1623228416 | bytes 6472192 | tf_op jit(solution)/shard_map/while/body/eval_jaxpr/rk,qkp->qrp/dot_general | solution.py:142
  430.0 4.8 reshape.236
  434.8 7.9 %pad.84 = f32[2,32,129,257]{3,2,1,0:T(8,128)} pad(f32[2,32,129,128]{3,2,1,0:T(8,128)} %reshape.236, f32[]{:T(128)} %constant.140.clone.1..sunk), padding=0_0x0_0x0_0x0_129 | pad | bytes 12714244 | tf_op jit(solution)/shard_map/while/body/eval_jaxpr/jit(_pad)/pad | solution.py:57
  442.8 11.6 %reshape.237 = f32[2,32,33153]{2,1,0:T(8,128)} reshape(f32[2,32,129,257]{3,2,1,0:T(8,128)} %pad.84) | data formatting | bytes 16974336 | tf_op jit(solution)/shard_map/while/body/eval_jaxpr/reshape | solution.py:58
  454.4 7.3 %pad.85 = f32[2,32,33280]{2,1,0:T(8,128)} pad(f32[2,32,33153]{2,1,0:T(8,128)} %reshape.237, f32[]{:T(128)} %constant.140.clone.1..sunk), padding=0_0x0_0x0_127 | pad | bytes 17006852 | tf_op jit(solution)/shard_map/while/body/eval_jaxpr/jit(_pad)/pad | solution.py:59
  461.7 9.4 %reshape.238 = f32[2,32,130,256]{3,2,1,0:T(8,128)} reshape(f32[2,32,33280]{2,1,0:T(8,128)} %pad.85) | data formatting | bytes 17039360 | tf_op jit(solution)/shard_map/while/body/eval_jaxpr/reshape | solution.py:60
  476.7 21.1 %all_to_all.46 = f32[8,2,2,32,256]{4,1,2,3,0:T(2,128)S(1)} all-to-all(f32[8,2,2,32,256]{4,1,2,3,0:T(2,128)S(1)} %broadcast_in_dim.45), channel_id=1, replica_groups=mesh['freq'=8,'space'=16] {'freq'}, dimensions={0} | all-to-all | bytes 2097152 | tf_op jit(solution)/shard_map/all_to_all | solution.py:26
  505.1 52.8 %all_to_all.47 = f32[128,32,256]{2,1,0:T(8,128)S(1)} all-to-all(f32[128,32,256]{2,1,0:T(8,128)S(1)} %copy.47), channel_id=1, replica_groups=mesh['freq'=8,'space'=16] {'space'}, dimensions={0} | all-to-all | bytes 8388608 | tf_op jit(solution)/shard_map/all_to_all | solution.py:153
  (86 shorter events, 73.1 us)
Async XLA Ops:
  13.2 70.0 %all-to-all-start = ((f32[8,512,256]{2,0,1:T(8,128)}), f32[8,512,256]{2,0,1:T(8,128)}, u32[]{:S(2)}, u32[]{:S(2)}) async-start(f32[8,512,256]{2,0,1:T(8,128)} %copy.35), calls=%async_computation | async-start | bytes 8388608 | tf_op jit(solution)/shard_map/all_to_all | solution.py:109
  21.8 61.3 %copy-start.4 = (f32[1,16,128]{2,1,0:T(8,128)}, f32[1,16,128]{2,1,0:T(8,128)S(1)}, u32[]{:S(2)}) copy-start(f32[1,16,128]{2,1,0:T(8,128)S(1)} %get-tuple-element.157) | copy-start | bytes 24580
  21.8 61.3 %copy-start.6 = (f32[1,16,128]{2,1,0:T(8,128)}, f32[1,16,128]{2,1,0:T(8,128)S(1)}, u32[]{:S(2)}) copy-start(f32[1,16,128]{2,1,0:T(8,128)S(1)} %get-tuple-element.158) | copy-start | bytes 24580
  87.1 24.6 %copy-start.1 = (f32[2,128,64]{1,2,0:T(8,128)S(1)}, f32[2,128,64]{1,2,0:T(8,128)}, u32[]{:S(2)}) copy-start(f32[2,128,64]{1,2,0:T(8,128)} %param.7) | copy-start | bytes 196612
  89.3 22.0 %all-to-all-start.1 = ((f32[8,2,2,32,256]{4,1,3,2,0:T(2,128)}), f32[8,2,2,32,256]{4,1,3,2,0:T(2,128)S(1)}, u32[]{:S(2)}, u32[]{:S(2)}) async-start(f32[8,2,2,32,256]{4,1,3,2,0:T(2,128)} %copy.37), calls=%async_computation.1 | async-start | bytes 2097152 | tf_op jit(solution)/shard_map/all_to_all | solution.py:20
  96.2 226.8 %all-reduce.5.cloned.1.call-start = ((), (), s32[]{:S(2)}) async-start(), calls=%async_computation.4 | async-start | bytes 786432 | tf_op jit(solution)/shard_map/psum | solution.py:124
  147.9 6.7 %copy-start = (f32[2,4128,128]{2,1,0:T(8,128)S(1)}, f32[2,4128,128]{2,1,0:T(8,128)}, u32[]{:S(2)}) copy-start(f32[2,4128,128]{2,1,0:T(8,128)} %reshape.235) | copy-start | bytes 12681220 | tf_op jit(solution)/shard_map/while
  204.7 6.7 %copy-start = (f32[2,4128,128]{2,1,0:T(8,128)S(1)}, f32[2,4128,128]{2,1,0:T(8,128)}, u32[]{:S(2)}) copy-start(f32[2,4128,128]{2,1,0:T(8,128)} %reshape.235) | copy-start | bytes 12681220 | tf_op jit(solution)/shard_map/while
  236.0 0.7 copy-start.2
  236.1 0.7 copy-start.3
  476.4 22.8 %copy-start.5 = (f32[1,16,128]{2,1,0:T(8,128)S(1)}, f32[1,16,128]{2,1,0:T(8,128)}, u32[]{:S(2)}) copy-start(f32[1,16,128]{2,1,0:T(8,128)} %copy-done.4) | copy-start | bytes 24580
  476.5 22.8 %copy-start.7 = (f32[1,16,128]{2,1,0:T(8,128)S(1)}, f32[1,16,128]{2,1,0:T(8,128)}, u32[]{:S(2)}) copy-start(f32[1,16,128]{2,1,0:T(8,128)} %copy-done.6) | copy-start | bytes 24580
Sparse Core Ops, SparseCore 0:
  236.9 85.9 all-reduce.4
where the time goes:
time: 577 us; the launch traced here: 567 us
  local copies, waits for them, and re-layouts  183 us (32%)
  waiting for transfers between devices  163 us (28%)
  blocking collectives  74 us (13%)
  other arithmetic  54 us (9%)
  matrix products  53.9 us (9%)
  starting transfers between devices  15.3 us (3%)
  between operations  13.9 us (2%)
  loops' own time  11 us (2%)
    psum x1, waiting for transfers between devices, body(): gram_sum, cross_sum = lax.psum((gram_raw, cross_raw), 'space')  86.1 us
    all_to_all x1, waiting for transfers between devices, body(): lax.all_to_all(traces, 'space', split_axis=1, concat_axis=0, tiled=True)  61.3 us
    all_to_all x1, blocking collectives, body(): lax.all_to_all(volume, 'space', split_axis=0, concat_axis=1, tiled=True)  52.8 us
    another operation x4, local copies, waits for them, and re-layouts, hankel(): tiled = jnp.tile(spectrum, (1, 1, window + 1))[:, :, :window * (width + 1)]  27.2 us
    reshape x2, local copies, waits for them, and re-layouts, hankel(): tiled.reshape(spectrum.shape[0], spectrum.shape[1], window, width + 1)  25.2 us
    another operation x4, other arithmetic, body(): lower_factor = jnp.linalg.cholesky(gram_matrix)  23.6 us
    reshape x2, local copies, waits for them, and re-layouts, diag_mean(): flat_rows = padded.reshape(halves, channels, window * (width + 1))  23.2 us
    all_to_all x1, blocking collectives, copy_for_each(): lax.all_to_all(jnp.broadcast_to(array[None], (peers, *array.shape)), axis...  21.1 us
  transfers between devices with their start and end apart: 3, of which 3 were waited for; matrix products, arithmetic and copies ran while one was open for 0% of the time, Pallas kernels for 0%

commit v1 on v0

v1 whole, which is shorter than its diff:
```python
import functools

import jax
import jax.numpy as jnp
from jax import lax
from jax.experimental import pallas as pl
from jax.experimental.pallas import tpu as pltpu
from jax.sharding import PartitionSpec as P

MESH = pl.DeviceIdType.MESH
F32 = jnp.float32
BF16 = jnp.bfloat16
NT = 1024
BAND_LO = 16
NF = 16
WIDTH = 256
COLS = 128
RANK = 64

AXES = ((0, 1, 2), (1, 2, 0), (2, 0, 1))
TILES = (3, 3, 2)
TILE_OFF = (0, 3, 6)
OFFSETS = ((2, 0), (2, 1), (1, 0), (3, 1), (3, 0), (1, 1), (0, 1))


def dot(a, b):
    return jnp.dot(a, b, preferred_element_type=F32, precision=lax.Precision.HIGHEST)


def dot_nt(a, b):
    return lax.dot_general(
        a, b, (((1,), (1,)), ((), ())), preferred_element_type=F32, precision=lax.Precision.HIGHEST
    )


def dot_tn(a, b):
    return lax.dot_general(
        a, b, (((0,), (0,)), ((), ())), preferred_element_type=F32, precision=lax.Precision.HIGHEST
    )


def iota(shape, dim):
    return lax.broadcasted_iota(jnp.int32, shape, dim)


def roll2(a, s):
    n = WIDTH
    return pltpu.roll(pltpu.roll(a, s % n, 0), s % n, 1)


def device(pos, core):
    x, y, z = pos
    return (2 * y + core, 4 * x + z)


def wave(part, pos, row_axis_is_time):
    shape = (64, 32) if row_axis_is_time else (32, 64)
    tdim, fdim = (0, 1) if row_axis_is_time else (1, 0)
    l = iota(shape, tdim)
    fq = iota(shape, fdim)
    a = AXES[part][0]
    moving = l // 16
    x, y, z = [moving if a == n else pos[n] for n in range(3)]
    t = 256 * y + 128 * ((l // 8) & 1) + 32 * x + 8 * z + (l & 7)
    k = BAND_LO + fq // 2
    phase = ((k * t) & (NT - 1)).astype(F32) * (2.0 * jnp.pi / NT)
    return jnp.where((fq & 1) == 0, jnp.cos(phase), -jnp.sin(phase))


def spread(table, rows, cols):
    up = (iota((rows, rows // 8), 0) // 8 == iota((rows, rows // 8), 1)).astype(F32)
    across = (iota((cols // 8, cols), 1) // 8 == iota((cols // 8, cols), 0)).astype(F32)
    wide = dot(up, dot(table, across))
    keep = (iota((rows, cols), 0) & 7) == (iota((rows, cols), 1) & 7)
    return jnp.where(keep, wide, 0.0)


def kernel(
    traces, probes, out,
    a0, a1, a2, fwd, inv_hi, inv_lo, b0, b1, b2, rb0, rb1, rb2, c0, c1, c2, rc0, rc1, rc2,
    own_probe, far_probe, rs_send, rs_recv, ag,
    d0, d1, d2, rd0, rd1, rd2, re0, re1, re2, g0, g1, g2,
    sa, ra, la, sb, rb, sc, rc, sp, rp, lp, srs, rrs, sag, rag, sd, rd, se, re_, sg, rg, lg,
):
    bufs_a, bufs_b, recv_b = (a0, a1, a2), (b0, b1, b2), (rb0, rb1, rb2)
    bufs_c, recv_c = (c0, c1, c2), (rc0, rc1, rc2)
    bufs_d, recv_d, recv_e, bufs_g = (d0, d1, d2), (rd0, rd1, rd2), (re0, re1, re2), (g0, g1, g2)
    f = lax.axis_index("freq")
    s = lax.axis_index("space")
    pos = (s // 4, f // 2, lax.rem(s, 4))
    core = lax.rem(f, 2)
    x, y, z = pos
    other = 1 - core

    def along(axis, step, flip=0):
        p = list(pos)
        p[axis] = lax.rem(p[axis] + step, 4)
        return device(p, lax.rem(core + flip, 2))

    def rotated(part, last):
        a, b, _ = AXES[part]
        return (pos[a], pos[b], last)

    def unrotated(part, last):
        a, b, c = AXES[part]
        p = [None] * 3
        p[a], p[b], p[c] = x, y, last
        return tuple(p)

    def is_me(p):
        return (p[0] == x) & (p[1] == y) & (p[2] == z)

    def remote(src, dst, ssem, rsem, dev):
        return pltpu.make_async_remote_copy(
            src_ref=src, dst_ref=dst, send_sem=ssem, recv_sem=rsem, device_id=dev, device_id_type=MESH
        )

    barrier = pltpu.get_barrier_semaphore()
    near = [along(axis, step, flip) for axis in range(3) for step in (1, 2, 3) for flip in (0, 1)]
    near.append(device(pos, other))
    for dev in near:
        pl.semaphore_signal(barrier, inc=1, device_id=dev, device_id_type=MESH)
    far = [fn(part, last) for part in (1, 2) for last in range(4) for fn in (rotated, unrotated)]
    for p in far:
        @pl.when(jnp.logical_not(is_me(p)))
        def _():
            pl.semaphore_signal(barrier, inc=1, device_id=device(p, core), device_id_type=MESH)

    local = []
    for part in range(3):
        a = AXES[part][0]
        me = 2 * pos[a] + core
        n = 8 * TILES[part]
        cp = pltpu.make_async_copy(
            traces.at[:, pl.ds(pl.multiple_of(64 * me + 8 * TILE_OFF[part], 8), n)],
            bufs_a[part].at[me], la.at[part],
        )
        cp.start()
        local.append(cp)
    own_cp = pltpu.make_async_copy(probes.at[lax.rem(z, 2)], own_probe, lp)
    own_cp.start()

    peers = len(near) + len(far)
    for p in far:
        peers = peers - is_me(p).astype(jnp.int32)
    pl.semaphore_wait(barrier, peers)

    sends_a = [[None] * 7 for _ in range(3)]
    for d, (step, flip) in enumerate(OFFSETS):
        for part in range(3):
            a = AXES[part][0]
            me = 2 * pos[a] + core
            to = 2 * lax.rem(pos[a] + step, 4) + lax.rem(core + flip, 2)
            n = 8 * TILES[part]
            cp = remote(
                traces.at[:, pl.ds(pl.multiple_of(64 * to + 8 * TILE_OFF[part], 8), n)],
                bufs_a[part].at[me], sa.at[part, d], ra.at[part, d], along(a, step, flip),
            )
            cp.start()
            sends_a[part][d] = cp
    probe_cp = remote(probes.at[lax.rem(z, 2)], far_probe, sp, rp, device(pos, other))
    probe_cp.start()

    for part in range(3):
        fwd[part] = spread(wave(part, pos, False) * (NT ** -0.5), 256, 512)
    for part in range(3):
        table = spread(wave(part, pos, True) * ((2.0 / NF) ** 0.5), 512, 256)
        hi = table.astype(BF16)
        inv_hi[part] = hi
        inv_lo[part] = (table - hi.astype(F32)).astype(BF16)

    sends_b = [[None] * 3 for _ in range(3)]
    for part in range(3):
        local[part].wait()
        for cp in sends_a[part]:
            cp.wait_recv()
        for tile in range(TILES[part]):
            block = bufs_a[part][:, :, 8 * tile : 8 * tile + 8, :].reshape(512, WIDTH)
            bufs_b[part][:, tile] = dot(fwd[part], block).reshape(4, 64, WIDTH)
        b = AXES[part][1]
        for d, step in enumerate((2, 1, 3)):
            to = lax.rem(pos[b] + step, 4)
            cp = remote(bufs_b[part].at[to], recv_b[part].at[d], sb.at[part, d], rb.at[part, d], along(b, step))
            cp.start()
            sends_b[part][d] = cp

    def send_rotated(buf_at, dst_at, ssem, rsem, part, goal, slot):
        for last in range(4):
            p = goal(part, last)
            me = is_me(p)
            cp = remote(buf_at(last), dst_at(slot), ssem.at[part, last], rsem.at[part, slot], device(p, core))
            lc = pltpu.make_async_copy(buf_at(last), dst_at(slot), rsem.at[part, slot])

            @pl.when(me)
            def _():
                lc.start()

            @pl.when(jnp.logical_not(me))
            def _():
                cp.start()

    def wait_rotated_send(buf_at, dst_at, ssem, rsem, part, goal, slot):
        for last in range(4):
            p = goal(part, last)
            cp = remote(buf_at(last), dst_at(slot), ssem.at[part, last], rsem.at[part, slot], device(p, core))

            @pl.when(jnp.logical_not(is_me(p)))
            def _():
                cp.wait_send()

    def wait_rotated_recv(dst_at, rsem, part):
        for last in range(4):
            pltpu.make_async_copy(dst_at(last), dst_at(last), rsem.at[part, last]).wait()

    for part in range(3):
        for cp in sends_b[part]:
            cp.wait_recv()
        b, c = AXES[part][1:]
        total = bufs_b[part][pos[b]] + recv_b[part][0] + recv_b[part][1] + recv_b[part][2]
        for last in range(4):
            bufs_c[part][last] = total[:, 16 * last : 16 * last + 16, :]
        send_rotated(
            lambda last: bufs_c[part].at[last], lambda slot: recv_c[part].at[slot], sc, rc, part, rotated, pos[c]
        )

    spec = []
    for part in range(3):
        wait_rotated_recv(lambda slot: recv_c[part].at[slot], rc, part)
        r = recv_c[part]
        spec.append(r[0] + r[1] + r[2] + r[3])
    spec = jnp.concatenate(spec, 0).reshape(8, 2, 8, WIDTH)
    re = spec[:, 0].reshape(64, WIDTH)
    im = spec[:, 1].reshape(64, WIDTH)
    both = jnp.concatenate([re, im], 0)
    turned = jnp.concatenate([im, -re], 0)
    own_cp.wait()
    probe_cp.wait_recv()
    probe = jnp.where(core == z // 2, own_probe[...], far_probe[...])
    probe_left = jnp.concatenate([probe, jnp.zeros_like(probe)], 1)
    probe_right = jnp.concatenate([jnp.zeros_like(probe), probe], 1)

    def window_sum(m):
        acc = m
        for step in (1, 2, 4, 8, 16, 32, 64):
            acc = acc + roll2(acc, WIDTH - step)
        return acc[:COLS, :COLS] + m[COLS:, COLS:]

    cov = jnp.concatenate([window_sum(dot_tn(both, both)), window_sum(dot_tn(both, turned))], 1)
    rs_send[...] = dot_tn(probe, cov).reshape(8, 8, 2 * COLS)

    me = 2 * x + core
    sends = []
    for d, (step, flip) in enumerate(OFFSETS):
        to = 2 * lax.rem(x + step, 4) + lax.rem(core + flip, 2)
        cp = remote(rs_send.at[to], rs_recv.at[d], srs.at[d], rrs.at[d], along(0, step, flip))
        cp.start()
        sends.append(cp)
    acc = rs_send[me]
    for d, cp in enumerate(sends):
        cp.wait_recv()
        acc = acc + rs_recv[d]
    ag[me] = acc
    gathers = []
    for d, (step, flip) in enumerate(OFFSETS):
        cp = remote(ag.at[me], ag.at[me], sag.at[d], rag.at[d], along(0, step, flip))
        cp.start()
        gathers.append(cp)
    for cp in gathers:
        cp.wait_recv()
    cross = ag[...].reshape(RANK, 2 * COLS)

    gram = dot(jnp.concatenate([cross[:, :COLS], cross[:, COLS:]], 0), probe_left)
    lane = iota((RANK, COLS), 1)
    row = iota((RANK, COLS), 0)
    ident = (lane == row + RANK).astype(F32)
    ar = gram[:RANK] + ident
    ai = gram[RANK:]
    tr = [ar[8 * n : 8 * n + 8] for n in range(8)]
    ti = [ai[8 * n : 8 * n + 8] for n in range(8)]
    below = iota((8, 1), 0)
    for k in range(RANK):
        t0, r0 = divmod(k, 8)
        row_r = tr[t0][r0 : r0 + 1, :]
        row_i = ti[t0][r0 : r0 + 1, :]
        scale = 1.0 / row_r[:, k : k + 1]
        row_r = row_r * scale
        row_i = row_i * scale
        for n in range(t0, 8):
            if n == t0 and r0 == 7:
                continue
            col_r = tr[n][:, k : k + 1]
            col_i = ti[n][:, k : k + 1]
            if n == t0:
                col_r = jnp.where(below > r0, col_r, 0.0)
                col_i = jnp.where(below > r0, col_i, 0.0)
            tr[n] = tr[n] - (col_r * row_r - col_i * row_i)
            ti[n] = ti[n] - (col_r * row_i + col_i * row_r)
    ar = jnp.concatenate(tr, 0)
    ai = jnp.concatenate(ti, 0)
    diag = jnp.sum(jnp.where(lane == row, ar, 0.0), axis=1, keepdims=True)
    scale = 1.0 / diag
    lhs = jnp.where(lane < RANK, pltpu.roll(ar, RANK, 1), ai) * scale
    swapped = jnp.concatenate([-cross[:, COLS:], cross[:, :COLS]], 1)
    fx = dot(lhs, jnp.concatenate([cross, swapped], 0))
    fx_turned = jnp.concatenate([fx[:, COLS:], -fx[:, :COLS]], 1)
    pe = dot_nt(probe_right, jnp.concatenate([ar, ai], 0))
    mix = dot(pe, jnp.concatenate([fx, fx_turned], 0))

    counts = iota((1, WIDTH), 1)
    counts = jnp.minimum(jnp.minimum(counts + 1, WIDTH - counts), COLS).astype(F32)
    share = 1.0 / counts

    def smear(m):
        m = jnp.concatenate([m, jnp.zeros_like(m)], 1)
        m = jnp.concatenate([m, jnp.zeros_like(m)], 0)
        acc = m
        for step in (1, 2, 4, 8, 16, 32, 64):
            acc = acc + roll2(acc, step)
        return (acc + roll2(m, COLS)) * share

    wr = smear(mix[:, :COLS])
    wi = smear(mix[:, COLS:])
    clean_re = dot(both, wr)
    clean_im = dot(both, wi)
    cre = (clean_re[:64] - clean_im[64:]).reshape(8, 1, 8, WIDTH)
    cim = (clean_re[64:] + clean_im[:64]).reshape(8, 1, 8, WIDTH)
    clean = jnp.concatenate([cre, cim], 1).reshape(8, 16, WIDTH)

    for part in range(3):
        bufs_d[part][...] = clean[TILE_OFF[part] : TILE_OFF[part] + TILES[part]]
        send_rotated(
            lambda last: bufs_d[part], lambda slot: recv_d[part].at[slot], sd, rd, part, unrotated, z
        )
    sends_e = [[None] * 3 for _ in range(3)]
    for part in range(3):
        wait_rotated_recv(lambda slot: recv_d[part].at[slot], rd, part)
        b = AXES[part][1]
        for d, step in enumerate((2, 1, 3)):
            cp = remote(recv_d[part], recv_e[part].at[pos[b]], se.at[part, d], re_.at[part, d], along(b, step))
            cp.start()
            sends_e[part][d] = cp
        recv_e[part][pos[b]] = recv_d[part][...]

    sends_g = [[None] * 7 for _ in range(3)]
    last_local = []
    for part in range(3):
        for cp in sends_e[part]:
            cp.wait_recv()
        for tile in range(TILES[part]):
            block = recv_e[part][:, :, tile].reshape(256, WIDTH)
            hi = block.astype(BF16)
            lo = (block - hi.astype(F32)).astype(BF16)
            th, tl = inv_hi[part], inv_lo[part]
            vol = jnp.dot(th, hi, preferred_element_type=F32)
            vol = vol + jnp.dot(th, lo, preferred_element_type=F32)
            vol = vol + jnp.dot(tl, hi, preferred_element_type=F32)
            bufs_g[part][:, :, 8 * tile : 8 * tile + 8, :] = vol.reshape(8, 8, 8, WIDTH)
        a = AXES[part][0]
        me = 2 * pos[a] + core
        n = 8 * TILES[part]
        here = pl.ds(pl.multiple_of(64 * me + 8 * TILE_OFF[part], 8), n)
        for d, (step, flip) in enumerate(OFFSETS):
            to = 2 * lax.rem(pos[a] + step, 4) + lax.rem(core + flip, 2)
            cp = remote(bufs_g[part].at[to], out.at[:, here], sg.at[part, d], rg.at[part, d], along(a, step, flip))
            cp.start()
            sends_g[part][d] = cp
        cp = pltpu.make_async_copy(bufs_g[part].at[me], out.at[:, here], lg.at[part])
        cp.start()
        last_local.append(cp)

    for part in range(3):
        for cp in sends_a[part]:
            cp.wait_send()
        for cp in sends_b[part]:
            cp.wait_send()
        c = AXES[part][2]
        wait_rotated_send(
            lambda last: bufs_c[part].at[last], lambda slot: recv_c[part].at[slot], sc, rc, part, rotated, pos[c]
        )
        wait_rotated_send(
            lambda last: bufs_d[part], lambda slot: recv_d[part].at[slot], sd, rd, part, unrotated, z
        )
        for cp in sends_e[part]:
            cp.wait_send()
    probe_cp.wait_send()
    for cp in sends + gathers:
        cp.wait_send()
    for part in range(3):
        last_local[part].wait()
        for cp in sends_g[part]:
            cp.wait()


def body(traces, probes):
    def vm(*shape, dtype=F32):
        return pltpu.VMEM(shape, dtype)

    def each(make):
        return [make(n) for n in TILES]

    dma = pltpu.SemaphoreType.DMA
    scratch = (
        each(lambda n: vm(8, 8, 8 * n, WIDTH))
        + [vm(3, 256, 512), vm(3, 512, 256, dtype=BF16), vm(3, 512, 256, dtype=BF16)]
        + each(lambda n: vm(4, n, 64, WIDTH))
        + each(lambda n: vm(3, n, 64, WIDTH))
        + each(lambda n: vm(4, n, 16, WIDTH))
        + each(lambda n: vm(4, n, 16, WIDTH))
        + [vm(COLS, RANK), vm(COLS, RANK), vm(8, 8, 256), vm(7, 8, 256), vm(8, 8, 256)]
        + each(lambda n: vm(n, 16, WIDTH))
        + each(lambda n: vm(4, n, 16, WIDTH))
        + each(lambda n: vm(4, 4, n, 16, WIDTH))
        + each(lambda n: vm(8, 8, 8 * n, WIDTH))
        + [
            dma((3, 7)), dma((3, 7)), dma((3,)),
            dma((3, 3)), dma((3, 3)),
            dma((3, 4)), dma((3, 4)),
            dma, dma, dma,
            dma((7,)), dma((7,)), dma((7,)), dma((7,)),
            dma((3, 4)), dma((3, 4)),
            dma((3, 3)), dma((3, 3)),
            dma((3, 7)), dma((3, 7)), dma((3,)),
        ]
    )
    return pl.pallas_call(
        kernel,
        out_shape=jax.ShapeDtypeStruct(traces.shape, F32),
        in_specs=[pl.BlockSpec(memory_space=pl.ANY)] * 2,
        out_specs=pl.BlockSpec(memory_space=pl.ANY),
        scratch_shapes=scratch,
        compiler_params=pltpu.CompilerParams(
            collective_id=0, has_side_effects=True, vmem_limit_bytes=56 << 20
        ),
    )(traces, probes)


def solution(mesh):
    in_specs = (P(("freq", "space"), None, None), P("freq", None, None))
    out_specs = P(("freq", "space"), None, None)
    return jax.shard_map(body, mesh=mesh, in_specs=in_specs, out_specs=out_specs, check_vma=False)
```

time: 577 us -> 126 us (0.22); the launches traced: 567 us -> 126 us
  local copies, waits for them, and re-layouts: 183 us -> 6.09 us
  waiting for transfers between devices: 163 us -> 0 us
  Pallas kernels: 0 us -> 120 us
  blocking collectives: 74 us -> 0 us
  other arithmetic: 54 us -> 0 us
  matrix products: 53.9 us -> 0 us
  starting transfers between devices: 15.3 us -> 0 us
  between operations: 13.9 us -> 0.01 us
  loops' own time: 11 us -> 0 us
    pallas_call x0 -> x1, Pallas kernels: none -> 120 us  [body(): pl.pallas_call(kernel, out_shape=jax.ShapeDtypeStruct(traces.shape, F32),...]
    reshape x13 -> x0, local copies, waits for them, and re-layouts: 89.5 us -> none  [the longest x2 25.2 us: hankel(): tiled.reshape(spectrum.shape[0], spectrum.shape[1], window, width + 1)]
    psum x1 -> x0, waiting for transfers between devices: 86.1 us -> none  [body(): gram_sum, cross_sum = lax.psum((gram_raw, cross_raw), 'space')]
    all_to_all x2 -> x0, waiting for transfers between devices: 76.4 us -> none  [the longest x1 61.3 us: body(): lax.all_to_all(traces, 'space', split_axis=1, concat_axis=0, tiled=True)]
    all_to_all x2 -> x0, blocking collectives: 74 us -> none  [the longest x1 52.8 us: body(): lax.all_to_all(volume, 'space', split_axis=0, concat_axis=1, tiled=True)]
    dot_general x10 -> x0, matrix products: 53.3 us -> none  [the longest x2 14.1 us: first_pass(): jnp.einsum('rk,qrp->qkp', sketch_basis, hankel_rows, precision=HIGHEST_PR...]
    another operation x9 -> x0, other arithmetic: 43.4 us -> none  [the longest x4 23.6 us: body(): lower_factor = jnp.linalg.cholesky(gram_matrix)]
    pad x4 -> x0, local copies, waits for them, and re-layouts: 30.5 us -> none  [the longest x2 15.8 us: diag_mean(): padded = jnp.pad(blocks, ((0, 0), (0, 0), (0, 0), (0, width + 1 - columns)))]
  transfers between devices with their start and end apart: 3 -> 0, of which waited for: 3 -> 0; matrix products, arithmetic and copies ran while one was open for 0% -> 0% of each run, Pallas kernels for 0% -> 0%
where the time goes in v1:
time: 126 us
  Pallas kernels  120 us (95%)
  local copies, waits for them, and re-layouts  6.09 us (5%)
    pallas_call x1, Pallas kernels, body(): pl.pallas_call(kernel, out_shape=jax.ShapeDtypeStruct(traces.shape, F32),...  120 us
    unnamed x2, local copies, waits for them, and re-layouts  6.09 us

profile of v1, /device:TPU:1, one launch (start us, length us, event | category | flops | bytes accessed | tf_op | source)
XLA Modules:
  0.0 126.0 jit_solution(12229959167077224404)
XLA Ops:
  0.0 1.6 %copy.3.probes = f32[2,128,64]{2,1,0:T(8,128)} copy(f32[2,128,64]{1,2,0:T(8,128)} %param.3) | data formatting | bytes 131072 | tf_op args[1]
  1.6 119.9 %shard_map.28 = f32[8,512,256]{2,1,0:T(8,128)} custom-call(f32[8,512,256]{2,1,0:T(8,128)} %traces.1, f32[2,128,64]{2,1,0:T(8,128)} %copy.3.probes), custom_call_target="tpu_custom_call" | custom-call | tf_op jit(solution)/shard_map/pallas_call | solution.py:425
  121.5 4.5 %copy.5 = f32[8,512,256]{2,1,0:T(8,128)} copy(f32[8,512,256]{2,1,0:T(8,128)} %shard_map.28) | data formatting | bytes 8388608

commit v2 on v1

v2 whole, which is shorter than its diff:
```python
import functools

import jax
import jax.numpy as jnp
from jax import lax
from jax.experimental import pallas as pl
from jax.experimental.pallas import tpu as pltpu
from jax.sharding import PartitionSpec as P

MESH = pl.DeviceIdType.MESH
F32 = jnp.float32
BF16 = jnp.bfloat16
NT = 1024
BAND_LO = 16
NF = 16
WIDTH = 256
COLS = 128
RANK = 64

AXES = ((0, 1, 2), (1, 2, 0), (2, 0, 1))
ORDER = ((0, 0), (1, 3), (2, 6), (0, 1), (1, 4), (2, 7), (0, 2), (1, 5))
BATCHES = (ORDER[:3], ORDER[3:6], ORDER[6:])
VMEM_LIMIT = 32
OFFSETS = ((2, 0), (2, 1), (1, 0), (3, 1), (3, 0), (1, 1), (0, 1))


def dot(a, b):
    return jnp.dot(a, b, preferred_element_type=F32, precision=lax.Precision.HIGHEST)


def dot_nt(a, b):
    return lax.dot_general(
        a, b, (((1,), (1,)), ((), ())), preferred_element_type=F32, precision=lax.Precision.HIGHEST
    )


def dot_tn(a, b):
    return lax.dot_general(
        a, b, (((0,), (0,)), ((), ())), preferred_element_type=F32, precision=lax.Precision.HIGHEST
    )


def iota(shape, dim):
    return lax.broadcasted_iota(jnp.int32, shape, dim)


def roll2(a, s):
    n = WIDTH
    return pltpu.roll(pltpu.roll(a, s % n, 0), s % n, 1)


def device(pos, core):
    x, y, z = pos
    return (2 * y + core, 4 * x + z)


def wave(part, pos, row_axis_is_time):
    shape = (64, 32) if row_axis_is_time else (32, 64)
    tdim, fdim = (0, 1) if row_axis_is_time else (1, 0)
    l = iota(shape, tdim)
    fq = iota(shape, fdim)
    a = AXES[part][0]
    moving = l // 16
    x, y, z = [moving if a == n else pos[n] for n in range(3)]
    t = 256 * y + 128 * ((l // 8) & 1) + 32 * x + 8 * z + (l & 7)
    m = fq // 2
    if part == 1:
        m = 4 * (m & 3) + m // 4
    k = BAND_LO + m
    phase = ((k * t) & (NT - 1)).astype(F32) * (2.0 * jnp.pi / NT)
    return jnp.where((fq & 1) == 0, jnp.cos(phase), -jnp.sin(phase))


def spread(table, rows, cols):
    up = (iota((rows, rows // 8), 0) // 8 == iota((rows, rows // 8), 1)).astype(F32)
    across = (iota((cols // 8, cols), 1) // 8 == iota((cols // 8, cols), 0)).astype(F32)
    wide = dot(up, dot(table, across))
    keep = (iota((rows, cols), 0) & 7) == (iota((rows, cols), 1) & 7)
    return jnp.where(keep, wide, 0.0)


def kernel(
    traces, probes, out,
    buf_a, fwd, inv_hi, inv_lo, buf_b, recv_b, buf_c, recv_c,
    own_probe, far_probe, rs_send, rs_recv, ag,
    buf_d, recv_d, recv_e, buf_g,
    sa, ra, la, sb, rb, sc, rc, sp, rp, lp, srs, rrs, sag, rag, sd, rd, se, re_, sg, rg, lg,
):
    f = lax.axis_index("freq")
    s = lax.axis_index("space")
    pos = (s // 4, f // 2, lax.rem(s, 4))
    core = lax.rem(f, 2)
    x, y, z = pos
    other = 1 - core
    home = [2 * pos[AXES[part][0]] + core for part in range(3)]

    def along(axis, step, flip=0):
        p = list(pos)
        p[axis] = lax.rem(p[axis] + step, 4)
        return device(p, lax.rem(core + flip, 2))

    def owner(part, last):
        a, b = pos[AXES[part][0]], pos[AXES[part][1]]
        if part == 0:
            return (a, b, last)
        turned = lax.rem(a + last, 4)
        return (turned, last, b) if part == 1 else (turned, b, last)

    index = (z, y, z)

    def member(part, last):
        a, b, c = AXES[part]
        p = [None] * 3
        p[a] = x if part == 0 else lax.rem(x + 4 - index[part], 4)
        p[b] = z if part == 1 else y
        p[c] = last
        return tuple(p)

    def is_me(p):
        return (p[0] == x) & (p[1] == y) & (p[2] == z)

    def remote(src, dst, ssem, rsem, dev):
        return pltpu.make_async_remote_copy(
            src_ref=src, dst_ref=dst, send_sem=ssem, recv_sem=rsem, device_id=dev, device_id_type=MESH
        )

    finish = []

    def begin(cp):
        cp.start()
        finish.append(cp.wait_send)
        return cp

    def to_four(buf_at, dst, ssem, rsem, goal):
        for last in range(4):
            p = goal(last)
            me = is_me(p)
            cp = remote(buf_at(last), dst, ssem.at[last], rsem, device(p, core))
            lc = pltpu.make_async_copy(buf_at(last), dst, rsem)

            @pl.when(me)
            def _():
                lc.start()

            @pl.when(jnp.logical_not(me))
            def _():
                cp.start()

            def wait(me=me, cp=cp):
                @pl.when(jnp.logical_not(me))
                def _():
                    cp.wait_send()

            finish.append(wait)

    def from_four(buf, rsem):
        for last in range(4):
            pltpu.make_async_copy(buf.at[last], buf.at[last], rsem.at[last]).wait()

    barrier = pltpu.get_barrier_semaphore()
    near = [along(axis, step, flip) for step in (2, 1, 3) for axis in range(3) for flip in (0, 1)]
    near.append(device(pos, other))
    for dev in near:
        pl.semaphore_signal(barrier, inc=1, device_id=dev, device_id_type=MESH)

    def channels(block, tile):
        return pl.ds(pl.multiple_of(64 * block + 8 * tile, 8), 8)

    local = {}
    for part, tile in ORDER:
        me = home[part]
        cp = pltpu.make_async_copy(traces.at[:, channels(me, tile)], buf_a.at[tile, me], la.at[tile])
        cp.start()
        local[tile] = cp
    own_cp = pltpu.make_async_copy(probes.at[lax.rem(z, 2)], own_probe, lp)
    own_cp.start()
    pl.semaphore_wait(barrier, len(near))

    sends_a = {tile: [] for _, tile in ORDER}
    for batch in BATCHES:
        for d, (step, flip) in enumerate(OFFSETS):
            for part, tile in batch:
                a = AXES[part][0]
                to = 2 * lax.rem(pos[a] + step, 4) + lax.rem(core + flip, 2)
                sends_a[tile].append(begin(remote(
                    traces.at[:, channels(to, tile)], buf_a.at[tile, home[part]],
                    sa.at[tile, d], ra.at[tile, d], along(a, step, flip),
                )))
    probe_cp = begin(remote(probes.at[lax.rem(z, 2)], far_probe, sp, rp, device(pos, other)))

    for part in range(3):
        fwd[part] = spread(wave(part, pos, False) * (NT ** -0.5), 256, 512)
    for part in range(3):
        table = spread(wave(part, pos, True) * ((2.0 / NF) ** 0.5), 512, 256)
        hi = table.astype(BF16)
        inv_hi[part] = hi
        inv_lo[part] = (table - hi.astype(F32)).astype(BF16)

    sends_b = {}
    for part, tile in ORDER:
        local[tile].wait()
        for cp in sends_a[tile]:
            cp.wait_recv()
        buf_b[tile] = dot(fwd[part], buf_a[tile].reshape(512, WIDTH)).reshape(4, 64, WIDTH)
        b = AXES[part][1]
        sends_b[tile] = [
            begin(remote(
                buf_b.at[tile, lax.rem(pos[b] + step, 4)], recv_b.at[tile, d],
                sb.at[tile, d], rb.at[tile, d], along(b, step),
            ))
            for d, step in enumerate((2, 1, 3))
        ]

    for part, tile in ORDER:
        for cp in sends_b[tile]:
            cp.wait_recv()
        b, c = AXES[part][1:]
        total = buf_b[tile, pos[b]] + recv_b[tile, 0] + recv_b[tile, 1] + recv_b[tile, 2]
        buf_c[tile] = total.reshape(4, 16, WIDTH)
        to_four(
            buf_c.at[tile].at.__getitem__, recv_c.at[tile, pos[c]], sc.at[tile], rc.at[tile, pos[c]],
            functools.partial(owner, part),
        )

    spec = []
    for tile in range(8):
        from_four(recv_c.at[tile], rc.at[tile])
    r = recv_c
    spec = (r[:, 0] + r[:, 1] + r[:, 2] + r[:, 3]).reshape(8, 2, 8, WIDTH)
    re = spec[:, 0].reshape(64, WIDTH)
    im = spec[:, 1].reshape(64, WIDTH)
    both = jnp.concatenate([re, im], 0)
    turned = jnp.concatenate([im, -re], 0)
    own_cp.wait()
    probe_cp.wait_recv()
    probe_t = jnp.where(core == z // 2, own_probe[...], far_probe[...])

    def window_sum(m):
        acc = m
        for step in (1, 2, 4, 8, 16, 32, 64):
            acc = acc + roll2(acc, WIDTH - step)
        return acc[:COLS, :COLS] + m[COLS:, COLS:]

    cov = jnp.concatenate([window_sum(dot_tn(both, both)), window_sum(dot_tn(both, turned))], 1)
    rs_send[...] = dot(probe_t, cov).reshape(8, 8, 2 * COLS)

    me = 2 * x + core
    sends = []
    for d, (step, flip) in enumerate(OFFSETS):
        to = 2 * lax.rem(x + step, 4) + lax.rem(core + flip, 2)
        sends.append(begin(remote(rs_send.at[to], rs_recv.at[d], srs.at[d], rrs.at[d], along(0, step, flip))))
    acc = rs_send[me]
    for d, cp in enumerate(sends):
        cp.wait_recv()
        acc = acc + rs_recv[d]
    ag[me] = acc
    gathers = [
        begin(remote(ag.at[me], ag.at[me], sag.at[d], rag.at[d], along(0, step, flip)))
        for d, (step, flip) in enumerate(OFFSETS)
    ]
    for cp in gathers:
        cp.wait_recv()
    cross = ag[...].reshape(RANK, 2 * COLS)

    none = jnp.zeros_like(probe_t)
    probe_top = jnp.concatenate([probe_t, none], 0)
    probe_low = jnp.concatenate([none, probe_t], 0)
    gram = dot_nt(jnp.concatenate([cross[:, :COLS], cross[:, COLS:]], 0), probe_top)
    lane = iota((RANK, COLS), 1)
    row = iota((RANK, COLS), 0)
    ident = (lane == row + RANK).astype(F32)
    ar = gram[:RANK] + ident
    ai = gram[RANK:]
    tr = [ar[8 * n : 8 * n + 8] for n in range(8)]
    ti = [ai[8 * n : 8 * n + 8] for n in range(8)]
    below = iota((8, 1), 0)
    for k in range(RANK):
        t0, r0 = divmod(k, 8)
        row_r = tr[t0][r0 : r0 + 1, :]
        row_i = ti[t0][r0 : r0 + 1, :]
        scale = 1.0 / row_r[:, k : k + 1]
        row_r = row_r * scale
        row_i = row_i * scale
        for n in range(t0, 8):
            if n == t0 and r0 == 7:
                continue
            col_r = tr[n][:, k : k + 1]
            col_i = ti[n][:, k : k + 1]
            if n == t0:
                col_r = jnp.where(below > r0, col_r, 0.0)
                col_i = jnp.where(below > r0, col_i, 0.0)
            tr[n] = tr[n] - (col_r * row_r - col_i * row_i)
            ti[n] = ti[n] - (col_r * row_i + col_i * row_r)
    ar = jnp.concatenate(tr, 0)
    ai = jnp.concatenate(ti, 0)
    diag = jnp.sum(jnp.where(lane == row, ar, 0.0), axis=1, keepdims=True)
    scale = 1.0 / diag
    lhs = jnp.where(lane < RANK, pltpu.roll(ar, RANK, 1), ai) * scale
    swapped = jnp.concatenate([-cross[:, COLS:], cross[:, :COLS]], 1)
    fx = dot(lhs, jnp.concatenate([cross, swapped], 0))
    fx_turned = jnp.concatenate([fx[:, COLS:], -fx[:, :COLS]], 1)
    pe = dot_nt(probe_low.T, jnp.concatenate([ar, ai], 0))
    mix = dot(pe, jnp.concatenate([fx, fx_turned], 0))

    counts = iota((1, WIDTH), 1)
    counts = jnp.minimum(jnp.minimum(counts + 1, WIDTH - counts), COLS).astype(F32)
    share = 1.0 / counts

    def smear(m):
        m = jnp.concatenate([m, jnp.zeros_like(m)], 1)
        m = jnp.concatenate([m, jnp.zeros_like(m)], 0)
        acc = m
        for step in (1, 2, 4, 8, 16, 32, 64):
            acc = acc + roll2(acc, step)
        return (acc + roll2(m, COLS)) * share

    wr = smear(mix[:, :COLS])
    wi = smear(mix[:, COLS:])
    clean_re = dot(both, wr)
    clean_im = dot(both, wi)
    cre = (clean_re[:64] - clean_im[64:]).reshape(8, 1, 8, WIDTH)
    cim = (clean_re[64:] + clean_im[:64]).reshape(8, 1, 8, WIDTH)
    clean = jnp.concatenate([cre, cim], 1).reshape(8, 16, WIDTH)

    for part, tile in ORDER:
        buf_d[tile] = clean[tile]
        to_four(
            lambda last: buf_d.at[tile], recv_d.at[tile, index[part]], sd.at[tile], rd.at[tile, index[part]],
            functools.partial(member, part),
        )
    sends_e = {}
    for part, tile in ORDER:
        from_four(recv_d.at[tile], rd.at[tile])
        b = AXES[part][1]
        sends_e[tile] = [
            begin(remote(recv_d.at[tile], recv_e.at[tile, pos[b]], se.at[tile, d], re_.at[tile, d], along(b, step)))
            for d, step in enumerate((2, 1, 3))
        ]
        recv_e[tile, pos[b]] = recv_d[tile]

    sends_g = []
    for part, tile in ORDER:
        for cp in sends_e[tile]:
            cp.wait_recv()
        block = recv_e[tile].reshape(256, WIDTH)
        hi = block.astype(BF16)
        lo = (block - hi.astype(F32)).astype(BF16)
        th, tl = inv_hi[part], inv_lo[part]
        vol = jnp.dot(th, hi, preferred_element_type=F32)
        vol = vol + jnp.dot(th, lo, preferred_element_type=F32)
        vol = vol + jnp.dot(tl, hi, preferred_element_type=F32)
        buf_g[tile] = vol.reshape(8, 8, 8, WIDTH)
        a = AXES[part][0]
        here = channels(home[part], tile)
        for d, (step, flip) in enumerate(OFFSETS):
            to = 2 * lax.rem(pos[a] + step, 4) + lax.rem(core + flip, 2)
            sends_g.append(begin(remote(
                buf_g.at[tile, to], out.at[:, here], sg.at[tile, d], rg.at[tile, d], along(a, step, flip)
            )))
        cp = pltpu.make_async_copy(buf_g.at[tile, home[part]], out.at[:, here], lg.at[tile])
        cp.start()
        finish.append(cp.wait)

    for cp in sends_g:
        cp.wait_recv()
    for wait in finish:
        wait()


def body(traces, probes):
    def vm(*shape, dtype=F32):
        return pltpu.VMEM(shape, dtype)

    dma = pltpu.SemaphoreType.DMA
    scratch = [
        vm(8, 8, 8, 8, WIDTH),
        vm(3, 256, 512), vm(3, 512, 256, dtype=BF16), vm(3, 512, 256, dtype=BF16),
        vm(8, 4, 64, WIDTH), vm(8, 3, 64, WIDTH),
        vm(8, 4, 16, WIDTH), vm(8, 4, 16, WIDTH),
        vm(RANK, COLS), vm(RANK, COLS), vm(8, 8, 256), vm(7, 8, 256), vm(8, 8, 256),
        vm(8, 16, WIDTH), vm(8, 4, 16, WIDTH), vm(8, 4, 4, 16, WIDTH),
        vm(8, 8, 8, 8, WIDTH),
        dma((8, 7)), dma((8, 7)), dma((8,)),
        dma((8, 3)), dma((8, 3)),
        dma((8, 4)), dma((8, 4)),
        dma, dma, dma,
        dma((7,)), dma((7,)), dma((7,)), dma((7,)),
        dma((8, 4)), dma((8, 4)),
        dma((8, 3)), dma((8, 3)),
        dma((8, 7)), dma((8, 7)), dma((8,)),
    ]
    return pl.pallas_call(
        kernel,
        out_shape=jax.ShapeDtypeStruct(traces.shape, F32),
        in_specs=[pl.BlockSpec(memory_space=pltpu.HBM), pl.BlockSpec(memory_space=pl.ANY)],
        out_specs=pl.BlockSpec(memory_space=pl.ANY),
        scratch_shapes=scratch,
        compiler_params=pltpu.CompilerParams(
            collective_id=0, has_side_effects=True, vmem_limit_bytes=VMEM_LIMIT << 20
        ),
    )(traces, jnp.swapaxes(probes, 1, 2))


def solution(mesh):
    in_specs = (P(("freq", "space"), None, None), P("freq", None, None))
    out_specs = P(("freq", "space"), None, None)
    return jax.shard_map(body, mesh=mesh, in_specs=in_specs, out_specs=out_specs, check_vma=False)
```

time: 126 us -> 108 us (0.86)
  Pallas kernels: 120 us -> 103 us
    pallas_call x1, Pallas kernels: 120 us -> 103 us  [body(): pl.pallas_call(kernel, out_shape=jax.ShapeDtypeStruct(traces.shape, F32),...]
    unnamed x2 -> x5, local copies, waits for them, and re-layouts: 6.09 us -> 5.04 us
where the time goes in v2:
time: 108 us
  Pallas kernels  103 us (95%)
  local copies, waits for them, and re-layouts  5.04 us (5%)
    pallas_call x1, Pallas kernels, body(): pl.pallas_call(kernel, out_shape=jax.ShapeDtypeStruct(traces.shape, F32),...  103 us
    unnamed x5, local copies, waits for them, and re-layouts  5.04 us

profile of v2, /device:TPU:1, one launch (start us, length us, event | category | flops | bytes accessed | tf_op | source)
XLA Modules:
  0.0 107.7 jit_solution(6112342466904054302)
XLA Ops:
  0.0 0.0 copy-start
  0.0 2.2 %copy-done = f32[8,512,256]{2,1,0:T(8,128)S(1)} copy-done((f32[8,512,256]{2,1,0:T(8,128)S(1)}, f32[8,512,256]{2,1,0:T(8,128)}, u32[]{:S(2)}) %copy-start) | copy-done | bytes 4194328
  2.2 0.0 copy-start.1
  2.2 0.8 copy-done.1
  3.0 102.7 %shard_map.28 = f32[8,512,256]{2,1,0:T(8,128)S(1)} custom-call(f32[8,512,256]{2,1,0:T(8,128)S(1)} %copy-done, f32[2,64,128]{2,1,0:T(8,128)S(1)} %bitcast.1), custom_call_target="tpu_custom_call" | custom-call | tf_op jit(solution)/shard_map/pallas_call | solution.py:392
  105.7 2.0 %copy.4 = f32[8,512,256]{2,1,0:T(8,128)} copy(f32[8,512,256]{2,1,0:T(8,128)S(1)} %shard_map.28) | data formatting | bytes 8388608
Async XLA Ops:
  0.0 2.2 %copy-start = (f32[8,512,256]{2,1,0:T(8,128)S(1)}, f32[8,512,256]{2,1,0:T(8,128)}, u32[]{:S(2)}) copy-start(f32[8,512,256]{2,1,0:T(8,128)} %traces.1) | copy-start | bytes 12582916
  2.2 0.8 copy-start.1

commit v3 on v2

--- a/solution.py
+++ b/solution.py
@@ -17,10 +17,13 @@
 COLS = 128
 RANK = 64
 
-AXES = ((0, 1, 2), (1, 2, 0), (2, 0, 1))
-ORDER = ((0, 0), (1, 3), (2, 6), (0, 1), (1, 4), (2, 7), (0, 2), (1, 5))
-BATCHES = (ORDER[:3], ORDER[3:6], ORDER[6:])
-VMEM_LIMIT = 32
+AXES = ((0, 1, 2), (0, 2, 1), (1, 2, 0), (2, 1, 0))
+KINDS = (0, 0, 1, 1, 2, 2, 3, 3)
+BATCHES = ((0, 4, 6), (2, 5, 7), (1,), (3,))
+ORDER = (0, 4, 6, 2, 5, 7, 1, 3)
+BACK = (0, 2, 1, 3, 4, 6, 5, 7)
+OFFSETS = ((2, 0), (2, 1), (1, 0), (3, 1), (3, 0), (1, 1), (0, 1))
+VMEM_LIMIT = 46
 OFFSETS = ((2, 0), (2, 1), (1, 0), (3, 1), (3, 0), (1, 1), (0, 1))
 
 
@@ -54,17 +57,17 @@
     return (2 * y + core, 4 * x + z)
 
 
-def wave(part, pos, row_axis_is_time):
+def wave(kind, pos, row_axis_is_time):
     shape = (64, 32) if row_axis_is_time else (32, 64)
     tdim, fdim = (0, 1) if row_axis_is_time else (1, 0)
     l = iota(shape, tdim)
     fq = iota(shape, fdim)
-    a = AXES[part][0]
+    a = AXES[kind][0]
     moving = l // 16
     x, y, z = [moving if a == n else pos[n] for n in range(3)]
     t = 256 * y + 128 * ((l // 8) & 1) + 32 * x + 8 * z + (l & 7)
     m = fq // 2
-    if part == 1:
+    if kind in (1, 2):
         m = 4 * (m & 3) + m // 4
     k = BAND_LO + m
     phase = ((k * t) & (NT - 1)).astype(F32) * (2.0 * jnp.pi / NT)
@@ -92,27 +95,26 @@
     core = lax.rem(f, 2)
     x, y, z = pos
     other = 1 - core
-    home = [2 * pos[AXES[part][0]] + core for part in range(3)]
+    home = [2 * pos[AXES[kind][0]] + core for kind in range(4)]
 
     def along(axis, step, flip=0):
         p = list(pos)
         p[axis] = lax.rem(p[axis] + step, 4)
         return device(p, lax.rem(core + flip, 2))
 
-    def owner(part, last):
-        a, b = pos[AXES[part][0]], pos[AXES[part][1]]
-        if part == 0:
-            return (a, b, last)
-        turned = lax.rem(a + last, 4)
-        return (turned, last, b) if part == 1 else (turned, b, last)
-
-    index = (z, y, z)
-
-    def member(part, last):
-        a, b, c = AXES[part]
+    def owner(kind, last):
+        a, b = pos[AXES[kind][0]], pos[AXES[kind][1]]
+        if kind > 1:
+            a = lax.rem(a + last, 4)
+        return (a, last, b) if kind in (1, 2) else (a, b, last)
+
+    index = (z, y, y, z)
+
+    def member(kind, last):
+        a, b, c = AXES[kind]
         p = [None] * 3
-        p[a] = x if part == 0 else lax.rem(x + 4 - index[part], 4)
-        p[b] = z if part == 1 else y
+        p[a] = x if kind < 2 else lax.rem(x + 4 - index[kind], 4)
+        p[b] = z if kind in (1, 2) else y
         p[c] = last
         return tuple(p)
 
@@ -167,8 +169,8 @@
         return pl.ds(pl.multiple_of(64 * block + 8 * tile, 8), 8)
 
     local = {}
-    for part, tile in ORDER:
-        me = home[part]
+    for tile in ORDER:
+        me = home[KINDS[tile]]
         cp = pltpu.make_async_copy(traces.at[:, channels(me, tile)], buf_a.at[tile, me], la.at[tile])
         cp.start()
         local[tile] = cp
@@ -176,33 +178,31 @@
     own_cp.start()
     pl.semaphore_wait(barrier, len(near))
 
-    sends_a = {tile: [] for _, tile in ORDER}
+    sends_a = {tile: [] for tile in ORDER}
     for batch in BATCHES:
         for d, (step, flip) in enumerate(OFFSETS):
-            for part, tile in batch:
-                a = AXES[part][0]
+            for tile in batch:
+                kind = KINDS[tile]
+                a = AXES[kind][0]
                 to = 2 * lax.rem(pos[a] + step, 4) + lax.rem(core + flip, 2)
                 sends_a[tile].append(begin(remote(
-                    traces.at[:, channels(to, tile)], buf_a.at[tile, home[part]],
+                    traces.at[:, channels(to, tile)], buf_a.at[tile, home[kind]],
                     sa.at[tile, d], ra.at[tile, d], along(a, step, flip),
                 )))
     probe_cp = begin(remote(probes.at[lax.rem(z, 2)], far_probe, sp, rp, device(pos, other)))
 
-    for part in range(3):
-        fwd[part] = spread(wave(part, pos, False) * (NT ** -0.5), 256, 512)
-    for part in range(3):
-        table = spread(wave(part, pos, True) * ((2.0 / NF) ** 0.5), 512, 256)
-        hi = table.astype(BF16)
-        inv_hi[part] = hi
-        inv_lo[part] = (table - hi.astype(F32)).astype(BF16)
+    for kind in range(4):
+        fwd[kind] = spread(wave(kind, pos, False) * (NT ** -0.5), 256, 512)
 
     sends_b = {}
-    for part, tile in ORDER:
+
+    def to_quads(tile):
+        kind = KINDS[tile]
         local[tile].wait()
         for cp in sends_a[tile]:
             cp.wait_recv()
-        buf_b[tile] = dot(fwd[part], buf_a[tile].reshape(512, WIDTH)).reshape(4, 64, WIDTH)
-        b = AXES[part][1]
+        buf_b[tile] = dot(fwd[kind], buf_a[tile].reshape(512, WIDTH)).reshape(4, 64, WIDTH)
+        b = AXES[kind][1]
         sends_b[tile] = [
             begin(remote(
                 buf_b.at[tile, lax.rem(pos[b] + step, 4)], recv_b.at[tile, d],
@@ -211,16 +211,32 @@
             for d, step in enumerate((2, 1, 3))
         ]
 
-    for part, tile in ORDER:
+    def to_owners(tile):
+        kind = KINDS[tile]
         for cp in sends_b[tile]:
             cp.wait_recv()
-        b, c = AXES[part][1:]
+        b, c = AXES[kind][1:]
         total = buf_b[tile, pos[b]] + recv_b[tile, 0] + recv_b[tile, 1] + recv_b[tile, 2]
         buf_c[tile] = total.reshape(4, 16, WIDTH)
         to_four(
             buf_c.at[tile].at.__getitem__, recv_c.at[tile, pos[c]], sc.at[tile], rc.at[tile, pos[c]],
-            functools.partial(owner, part),
+            functools.partial(owner, kind),
         )
+
+    for n, batch in enumerate(BATCHES):
+        for tile in batch:
+            to_quads(tile)
+        if n == 2:
+            for kind in range(4):
+                table = spread(wave(kind, pos, True) * ((2.0 / NF) ** 0.5), 512, 256)
+                hi = table.astype(BF16)
+                inv_hi[kind] = hi
+                inv_lo[kind] = (table - hi.astype(F32)).astype(BF16)
+        if n:
+            for tile in BATCHES[n - 1]:
+                to_owners(tile)
+    for tile in BATCHES[-1]:
+        to_owners(tile)
 
     spec = []
     for tile in range(8):
@@ -322,16 +338,18 @@
     cim = (clean_re[64:] + clean_im[:64]).reshape(8, 1, 8, WIDTH)
     clean = jnp.concatenate([cre, cim], 1).reshape(8, 16, WIDTH)
 
-    for part, tile in ORDER:
+    for tile in BACK:
+        kind = KINDS[tile]
         buf_d[tile] = clean[tile]
         to_four(
-            lambda last: buf_d.at[tile], recv_d.at[tile, index[part]], sd.at[tile], rd.at[tile, index[part]],
-            functools.partial(member, part),
+            lambda last: buf_d.at[tile], recv_d.at[tile, index[kind]], sd.at[tile], rd.at[tile, index[kind]],
+            functools.partial(member, kind),
         )
     sends_e = {}
-    for part, tile in ORDER:
+    for tile in BACK:
+        kind = KINDS[tile]
         from_four(recv_d.at[tile], rd.at[tile])
-        b = AXES[part][1]
+        b = AXES[kind][1]
         sends_e[tile] = [
             begin(remote(recv_d.at[tile], recv_e.at[tile, pos[b]], se.at[tile, d], re_.at[tile, d], along(b, step)))
             for d, step in enumerate((2, 1, 3))
@@ -339,25 +357,26 @@
         recv_e[tile, pos[b]] = recv_d[tile]
 
     sends_g = []
-    for part, tile in ORDER:
+    for tile in BACK:
+        kind = KINDS[tile]
         for cp in sends_e[tile]:
             cp.wait_recv()
         block = recv_e[tile].reshape(256, WIDTH)
         hi = block.astype(BF16)
         lo = (block - hi.astype(F32)).astype(BF16)
-        th, tl = inv_hi[part], inv_lo[part]
+        th, tl = inv_hi[kind], inv_lo[kind]
         vol = jnp.dot(th, hi, preferred_element_type=F32)
         vol = vol + jnp.dot(th, lo, preferred_element_type=F32)
         vol = vol + jnp.dot(tl, hi, preferred_element_type=F32)
         buf_g[tile] = vol.reshape(8, 8, 8, WIDTH)
-        a = AXES[part][0]
-        here = channels(home[part], tile)
+        a = AXES[kind][0]
+        here = channels(home[kind], tile)
         for d, (step, flip) in enumerate(OFFSETS):
             to = 2 * lax.rem(pos[a] + step, 4) + lax.rem(core + flip, 2)
             sends_g.append(begin(remote(
                 buf_g.at[tile, to], out.at[:, here], sg.at[tile, d], rg.at[tile, d], along(a, step, flip)
             )))
-        cp = pltpu.make_async_copy(buf_g.at[tile, home[part]], out.at[:, here], lg.at[tile])
+        cp = pltpu.make_async_copy(buf_g.at[tile, home[kind]], out.at[:, here], lg.at[tile])
         cp.start()
         finish.append(cp.wait)
 
@@ -374,7 +393,7 @@
     dma = pltpu.SemaphoreType.DMA
     scratch = [
         vm(8, 8, 8, 8, WIDTH),
-        vm(3, 256, 512), vm(3, 512, 256, dtype=BF16), vm(3, 512, 256, dtype=BF16),
+        vm(4, 256, 512), vm(4, 512, 256, dtype=BF16), vm(4, 512, 256, dtype=BF16),
         vm(8, 4, 64, WIDTH), vm(8, 3, 64, WIDTH),
         vm(8, 4, 16, WIDTH), vm(8, 4, 16, WIDTH),
         vm(RANK, COLS), vm(RANK, COLS), vm(8, 8, 256), vm(7, 8, 256), vm(8, 8, 256),

time: 108 us -> 102 us (0.944)
  Pallas kernels: 103 us -> 98.6 us
  local copies, waits for them, and re-layouts: 5.04 us -> 2.85 us
    pallas_call x1, Pallas kernels: 103 us -> 98.6 us  [body(): pl.pallas_call(kernel, out_shape=jax.ShapeDtypeStruct(traces.shape, F32),...]
    unnamed x5 -> x3, local copies, waits for them, and re-layouts: 5.04 us -> 2.85 us
where the time goes in v3:
time: 102 us; the launch traced here: 101 us
  Pallas kernels  98.6 us (97%)
  local copies, waits for them, and re-layouts  2.85 us (3%)
    pallas_call x1, Pallas kernels, body(): pl.pallas_call(kernel, out_shape=jax.ShapeDtypeStruct(traces.shape, F32),...  98.6 us
    unnamed x3, local copies, waits for them, and re-layouts  2.85 us

profile of v3, /device:TPU:1, one launch (start us, length us, event | category | flops | bytes accessed | tf_op | source)
XLA Modules:
  0.0 101.5 jit_solution(3167225138142980036)
XLA Ops:
  0.0 0.0 copy-start
  0.0 0.8 copy-done
  0.8 98.6 %shard_map.28 = f32[8,512,256]{2,1,0:T(8,128)S(1)} custom-call(f32[8,512,256]{2,1,0:T(8,128)} %traces.1, f32[2,64,128]{2,1,0:T(8,128)S(1)} %bitcast.1), custom_call_target="tpu_custom_call" | custom-call | tf_op jit(solution)/shard_map/pallas_call | solution.py:411
  99.5 2.0 %copy.4 = f32[8,512,256]{2,1,0:T(8,128)} copy(f32[8,512,256]{2,1,0:T(8,128)S(1)} %shard_map.28) | data formatting | bytes 8388608
Async XLA Ops:
  0.0 0.8 copy-start

commit v4 on v3

--- a/solution.py
+++ b/solution.py
@@ -21,6 +21,10 @@
 KINDS = (0, 0, 1, 1, 2, 2, 3, 3)
 BATCHES = ((0, 4, 6), (2, 5, 7), (1,), (3,))
 ORDER = (0, 4, 6, 2, 5, 7, 1, 3)
+LAST = 3
+PLANE = tuple(
+    (dy, dz) for dy in (2, 1, 3, 0) for dz in (2, 1, 3, 0) if (dy, dz) != (0, 0)
+)
 BACK = (0, 2, 1, 3, 4, 6, 5, 7)
 OFFSETS = ((2, 0), (2, 1), (1, 0), (3, 1), (3, 0), (1, 1), (0, 1))
 VMEM_LIMIT = 46
@@ -84,10 +88,10 @@
 
 def kernel(
     traces, probes, out,
-    buf_a, fwd, inv_hi, inv_lo, buf_b, recv_b, buf_c, recv_c,
-    own_probe, far_probe, rs_send, rs_recv, ag,
+    buf_a, fwd, inv_hi, inv_lo, buf_b, recv_b, buf_c, recv_c, recv_x,
+    own_probe, far_probe, rs_send, rs_recv, ag, half, fr, fi,
     buf_d, recv_d, recv_e, buf_g,
-    sa, ra, la, sb, rb, sc, rc, sp, rp, lp, srs, rrs, sag, rag, sd, rd, se, re_, sg, rg, lg,
+    sa, ra, la, sb, rb, sc, rc, sx, rx, sp, rp, lp, srs, rrs, sag, rag, sd, rd, se, re_, sg, rg, lg,
 ):
     f = lax.axis_index("freq")
     s = lax.axis_index("space")
@@ -195,6 +199,7 @@
         fwd[kind] = spread(wave(kind, pos, False) * (NT ** -0.5), 256, 512)
 
     sends_b = {}
+    direct = []
 
     def to_quads(tile):
         kind = KINDS[tile]
@@ -202,6 +207,14 @@
         for cp in sends_a[tile]:
             cp.wait_recv()
         buf_b[tile] = dot(fwd[kind], buf_a[tile].reshape(512, WIDTH)).reshape(4, 64, WIDTH)
+        if tile == LAST:
+            for d, (dy, dz) in enumerate(PLANE):
+                ty, tz = lax.rem(y + dy, 4), lax.rem(z + dz, 4)
+                rows = pl.ds(pl.multiple_of(16 * ty, 16), 16)
+                direct.append(begin(remote(
+                    buf_b.at[LAST, tz, rows], recv_x.at[d], sx.at[d], rx.at[d], device((x, ty, tz), core)
+                )))
+            return
         b = AXES[kind][1]
         sends_b[tile] = [
             begin(remote(
@@ -235,14 +248,23 @@
         if n:
             for tile in BATCHES[n - 1]:
                 to_owners(tile)
-    for tile in BATCHES[-1]:
-        to_owners(tile)
-
-    spec = []
+
     for tile in range(8):
-        from_four(recv_c.at[tile], rc.at[tile])
+        if tile != LAST:
+            from_four(recv_c.at[tile], rc.at[tile])
+    last = buf_b[LAST, z, pl.ds(pl.multiple_of(16 * y, 16), 16), :]
+    for d, cp in enumerate(direct):
+        cp.wait_recv()
+        last = last + recv_x[d]
     r = recv_c
-    spec = (r[:, 0] + r[:, 1] + r[:, 2] + r[:, 3]).reshape(8, 2, 8, WIDTH)
+    spec = jnp.concatenate(
+        [
+            r[:LAST, 0] + r[:LAST, 1] + r[:LAST, 2] + r[:LAST, 3],
+            last[None],
+            r[LAST + 1 :, 0] + r[LAST + 1 :, 1] + r[LAST + 1 :, 2] + r[LAST + 1 :, 3],
+        ],
+        0,
+    ).reshape(8, 2, 8, WIDTH)
     re = spec[:, 0].reshape(64, WIDTH)
     im = spec[:, 1].reshape(64, WIDTH)
     both = jnp.concatenate([re, im], 0)
@@ -258,24 +280,20 @@
         return acc[:COLS, :COLS] + m[COLS:, COLS:]
 
     cov = jnp.concatenate([window_sum(dot_tn(both, both)), window_sum(dot_tn(both, turned))], 1)
-    rs_send[...] = dot(probe_t, cov).reshape(8, 8, 2 * COLS)
-
-    me = 2 * x + core
-    sends = []
-    for d, (step, flip) in enumerate(OFFSETS):
-        to = 2 * lax.rem(x + step, 4) + lax.rem(core + flip, 2)
-        sends.append(begin(remote(rs_send.at[to], rs_recv.at[d], srs.at[d], rrs.at[d], along(0, step, flip))))
-    acc = rs_send[me]
-    for d, cp in enumerate(sends):
+    rs_send[...] = dot(probe_t, cov).reshape(2, 32, 2 * COLS)
+
+    swap = begin(remote(rs_send.at[other], rs_recv.at[3], srs.at[3], rrs.at[3], device(pos, other)))
+    swap.wait_recv()
+    half[...] = rs_send[core] + rs_recv[3]
+    sends = [
+        begin(remote(half, rs_recv.at[d], srs.at[d], rrs.at[d], along(0, step)))
+        for d, step in enumerate((2, 1, 3))
+    ]
+    for cp in sends:
         cp.wait_recv()
-        acc = acc + rs_recv[d]
-    ag[me] = acc
-    gathers = [
-        begin(remote(ag.at[me], ag.at[me], sag.at[d], rag.at[d], along(0, step, flip)))
-        for d, (step, flip) in enumerate(OFFSETS)
-    ]
-    for cp in gathers:
-        cp.wait_recv()
+    ag[core] = half[...] + rs_recv[0] + rs_recv[1] + rs_recv[2]
+    gather = begin(remote(ag.at[core], ag.at[core], sag, rag, device(pos, other)))
+    gather.wait_recv()
     cross = ag[...].reshape(RANK, 2 * COLS)
 
     none = jnp.zeros_like(probe_t)
@@ -290,28 +308,39 @@
     tr = [ar[8 * n : 8 * n + 8] for n in range(8)]
     ti = [ai[8 * n : 8 * n + 8] for n in range(8)]
     below = iota((8, 1), 0)
-    for k in range(RANK):
+    for k in range(0, RANK, 2):
         t0, r0 = divmod(k, 8)
-        row_r = tr[t0][r0 : r0 + 1, :]
-        row_i = ti[t0][r0 : r0 + 1, :]
-        scale = 1.0 / row_r[:, k : k + 1]
-        row_r = row_r * scale
-        row_i = row_i * scale
+        p1r, p1i = tr[t0][r0 : r0 + 1, :], ti[t0][r0 : r0 + 1, :]
+        p2r, p2i = tr[t0][r0 + 1 : r0 + 2, :], ti[t0][r0 + 1 : r0 + 2, :]
+        d1 = jnp.broadcast_to(p1r[:, k : k + 1], (1, COLS))
+        er = jnp.broadcast_to(p1r[:, k + 1 : k + 2], (1, COLS))
+        ei = jnp.broadcast_to(p1i[:, k + 1 : k + 2], (1, COLS))
+        d2 = jnp.broadcast_to(p2r[:, k + 1 : k + 2], (1, COLS))
+        inv1 = 1.0 / d1
+        gr, gi = er * inv1, ei * inv1
+        inv2 = 1.0 / (d2 - (er * gr + ei * gi))
+        u2r = (p2r - (gr * p1r + gi * p1i)) * inv2
+        u2i = (p2i - (gr * p1i - gi * p1r)) * inv2
+        u1r = p1r * inv1 - (gr * u2r - gi * u2i)
+        u1i = p1i * inv1 - (gr * u2i + gi * u2r)
+        fr[k : k + 1, :] = u1r
+        fi[k : k + 1, :] = u1i
+        fr[k + 1 : k + 2, :] = u2r
+        fi[k + 1 : k + 2, :] = u2i
         for n in range(t0, 8):
-            if n == t0 and r0 == 7:
+            if n == t0 and r0 == 6:
                 continue
-            col_r = tr[n][:, k : k + 1]
-            col_i = ti[n][:, k : k + 1]
+            c1r, c1i = tr[n][:, k : k + 1], ti[n][:, k : k + 1]
+            c2r, c2i = tr[n][:, k + 1 : k + 2], ti[n][:, k + 1 : k + 2]
             if n == t0:
-                col_r = jnp.where(below > r0, col_r, 0.0)
-                col_i = jnp.where(below > r0, col_i, 0.0)
-            tr[n] = tr[n] - (col_r * row_r - col_i * row_i)
-            ti[n] = ti[n] - (col_r * row_i + col_i * row_r)
+                c1r, c1i, c2r, c2i = [jnp.where(below > r0 + 1, c, 0.0) for c in (c1r, c1i, c2r, c2i)]
+            tr[n], ti[n] = (
+                tr[n] - ((c1r * u1r - c1i * u1i) + (c2r * u2r - c2i * u2i)),
+                ti[n] - ((c1r * u1i + c1i * u1r) + (c2r * u2i + c2i * u2r)),
+            )
     ar = jnp.concatenate(tr, 0)
     ai = jnp.concatenate(ti, 0)
-    diag = jnp.sum(jnp.where(lane == row, ar, 0.0), axis=1, keepdims=True)
-    scale = 1.0 / diag
-    lhs = jnp.where(lane < RANK, pltpu.roll(ar, RANK, 1), ai) * scale
+    lhs = jnp.where(lane < RANK, pltpu.roll(fr[...], RANK, 1), fi[...])
     swapped = jnp.concatenate([-cross[:, COLS:], cross[:, :COLS]], 1)
     fx = dot(lhs, jnp.concatenate([cross, swapped], 0))
     fx_turned = jnp.concatenate([fx[:, COLS:], -fx[:, :COLS]], 1)
@@ -395,15 +424,16 @@
         vm(8, 8, 8, 8, WIDTH),
         vm(4, 256, 512), vm(4, 512, 256, dtype=BF16), vm(4, 512, 256, dtype=BF16),
         vm(8, 4, 64, WIDTH), vm(8, 3, 64, WIDTH),
-        vm(8, 4, 16, WIDTH), vm(8, 4, 16, WIDTH),
-        vm(RANK, COLS), vm(RANK, COLS), vm(8, 8, 256), vm(7, 8, 256), vm(8, 8, 256),
+        vm(8, 4, 16, WIDTH), vm(8, 4, 16, WIDTH), vm(15, 16, WIDTH),
+        vm(RANK, COLS), vm(RANK, COLS), vm(2, 32, 256), vm(4, 32, 256), vm(2, 32, 256), vm(32, 256),
+        vm(RANK, COLS), vm(RANK, COLS),
         vm(8, 16, WIDTH), vm(8, 4, 16, WIDTH), vm(8, 4, 4, 16, WIDTH),
         vm(8, 8, 8, 8, WIDTH),
         dma((8, 7)), dma((8, 7)), dma((8,)),
         dma((8, 3)), dma((8, 3)),
-        dma((8, 4)), dma((8, 4)),
+        dma((8, 4)), dma((8, 4)), dma((15,)), dma((15,)),
         dma, dma, dma,
-        dma((7,)), dma((7,)), dma((7,)), dma((7,)),
+        dma((4,)), dma((4,)), dma, dma,
         dma((8, 4)), dma((8, 4)),
         dma((8, 3)), dma((8, 3)),
         dma((8, 7)), dma((8, 7)), dma((8,)),

time: 102 us -> 95.5 us (0.936)
  Pallas kernels: 98.6 us -> 92.5 us
    pallas_call x1, Pallas kernels: 98.6 us -> 92.5 us  [body(): pl.pallas_call(kernel, out_shape=jax.ShapeDtypeStruct(traces.shape, F32),...]
where the time goes in v4:
time: 95.5 us; the launch traced here: 95.3 us
  Pallas kernels  92.5 us (97%)
  local copies, waits for them, and re-layouts  2.85 us (3%)
    pallas_call x1, Pallas kernels, body(): pl.pallas_call(kernel, out_shape=jax.ShapeDtypeStruct(traces.shape, F32),...  92.5 us
    unnamed x3, local copies, waits for them, and re-layouts  2.85 us

profile of v4, /device:TPU:1, one launch (start us, length us, event | category | flops | bytes accessed | tf_op | source)
XLA Modules:
  0.0 95.3 jit_solution(4249189489146575870)
XLA Ops:
  0.0 0.0 copy-start
  0.0 0.8 copy-done
  0.8 92.5 %shard_map.28 = f32[8,512,256]{2,1,0:T(8,128)S(1)} custom-call(f32[8,512,256]{2,1,0:T(8,128)} %traces.1, f32[2,64,128]{2,1,0:T(8,128)S(1)} %bitcast.1), custom_call_target="tpu_custom_call" | custom-call | tf_op jit(solution)/shard_map/pallas_call | solution.py:441
  93.3 2.0 %copy.4 = f32[8,512,256]{2,1,0:T(8,128)} copy(f32[8,512,256]{2,1,0:T(8,128)S(1)} %shard_map.28) | data formatting | bytes 8388608
Async XLA Ops:
  0.0 0.8 copy-start

commit v5 on v4

--- a/solution.py
+++ b/solution.py
@@ -25,7 +25,7 @@
 PLANE = tuple(
     (dy, dz) for dy in (2, 1, 3, 0) for dz in (2, 1, 3, 0) if (dy, dz) != (0, 0)
 )
-BACK = (0, 2, 1, 3, 4, 6, 5, 7)
+BACK = (0, 2, 4, 6, 5, 7, 1, 3)
 OFFSETS = ((2, 0), (2, 1), (1, 0), (3, 1), (3, 0), (1, 1), (0, 1))
 VMEM_LIMIT = 46
 OFFSETS = ((2, 0), (2, 1), (1, 0), (3, 1), (3, 0), (1, 1), (0, 1))
@@ -252,26 +252,30 @@
     for tile in range(8):
         if tile != LAST:
             from_four(recv_c.at[tile], rc.at[tile])
+    own_cp.wait()
+    probe_cp.wait_recv()
+    probe_t = jnp.where(core == z // 2, own_probe[...], far_probe[...])
+    r = recv_c
+
+    def turn(m):
+        m = m.reshape(-1, 2, 8, WIDTH)
+        return jnp.concatenate([m[:, 1:], -m[:, :1]], 1).reshape(-1, WIDTH)
+
+    low = r[:LAST, 0] + r[:LAST, 1] + r[:LAST, 2] + r[:LAST, 3]
+    high = r[LAST + 1 :, 0] + r[LAST + 1 :, 1] + r[LAST + 1 :, 2] + r[LAST + 1 :, 3]
+    early = jnp.concatenate([low, high], 0).reshape(-1, WIDTH)
+    part_re = dot_tn(early, early)
+    part_im = dot_tn(early, turn(early))
     last = buf_b[LAST, z, pl.ds(pl.multiple_of(16 * y, 16), 16), :]
     for d, cp in enumerate(direct):
         cp.wait_recv()
         last = last + recv_x[d]
-    r = recv_c
-    spec = jnp.concatenate(
-        [
-            r[:LAST, 0] + r[:LAST, 1] + r[:LAST, 2] + r[:LAST, 3],
-            last[None],
-            r[LAST + 1 :, 0] + r[LAST + 1 :, 1] + r[LAST + 1 :, 2] + r[LAST + 1 :, 3],
-        ],
-        0,
-    ).reshape(8, 2, 8, WIDTH)
+    cov_re = part_re + dot_tn(last, last)
+    cov_im = part_im + dot_tn(last, turn(last))
+    spec = jnp.concatenate([low, last[None], high], 0).reshape(8, 2, 8, WIDTH)
     re = spec[:, 0].reshape(64, WIDTH)
     im = spec[:, 1].reshape(64, WIDTH)
     both = jnp.concatenate([re, im], 0)
-    turned = jnp.concatenate([im, -re], 0)
-    own_cp.wait()
-    probe_cp.wait_recv()
-    probe_t = jnp.where(core == z // 2, own_probe[...], far_probe[...])
 
     def window_sum(m):
         acc = m
@@ -279,7 +283,7 @@
             acc = acc + roll2(acc, WIDTH - step)
         return acc[:COLS, :COLS] + m[COLS:, COLS:]
 
-    cov = jnp.concatenate([window_sum(dot_tn(both, both)), window_sum(dot_tn(both, turned))], 1)
+    cov = jnp.concatenate([window_sum(cov_re), window_sum(cov_im)], 1)
     rs_send[...] = dot(probe_t, cov).reshape(2, 32, 2 * COLS)
 
     swap = begin(remote(rs_send.at[other], rs_recv.at[3], srs.at[3], rrs.at[3], device(pos, other)))

time: 95.5 us -> 95.6 us (level)
  no operation moved by 1% of the time
where the time goes in v5:
time: 95.6 us; the launch traced here: 95.5 us
  Pallas kernels  92.6 us (97%)
  local copies, waits for them, and re-layouts  2.85 us (3%)
    pallas_call x1, Pallas kernels, body(): pl.pallas_call(kernel, out_shape=jax.ShapeDtypeStruct(traces.shape, F32),...  92.6 us
    unnamed x3, local copies, waits for them, and re-layouts  2.85 us

profile of v5, /device:TPU:1, one launch (start us, length us, event | category | flops | bytes accessed | tf_op | source)
XLA Modules:
  0.0 95.5 jit_solution(4336736258837743258)
XLA Ops:
  0.0 0.0 copy-start
  0.0 0.8 copy-done
  0.8 92.6 %shard_map.28 = f32[8,512,256]{2,1,0:T(8,128)S(1)} custom-call(f32[8,512,256]{2,1,0:T(8,128)} %traces.1, f32[2,64,128]{2,1,0:T(8,128)S(1)} %bitcast.1), custom_call_target="tpu_custom_call" | custom-call | tf_op jit(solution)/shard_map/pallas_call | solution.py:445
  93.5 2.0 %copy.4 = f32[8,512,256]{2,1,0:T(8,128)} copy(f32[8,512,256]{2,1,0:T(8,128)S(1)} %shard_map.28) | data formatting | bytes 8388608
Async XLA Ops:
  0.0 0.8 copy-start
